TPU v7x, 256 devices: a whole 4x4x8 slice. The times are simulated.
256 devices in a mesh: lon: 16 (over x_hi, z), lat: 8 (over x_lo, y), img: 2 (over core).
Axes of the slice: x: 4 (x_hi: 2, x_lo: 2; x = x_hi * 2 + x_lo), y: 4, z: 8, core: 2. Of those that a mesh axis runs over, the one named last changes fastest.
Arguments:
- control: bfloat16 [2, 128, 256, 320], P('img', 'lat', 'lon'), may hold values from -6 to 6
- conv_weight: bfloat16 [3, 3, 320, 320], replicated, may hold values from -0.109375 to 0.109375
- conv_bias: float32 [320], replicated, may hold values from -3 to 3
- zero_weight: bfloat16 [320, 320], replicated, may hold values from -0.3125 to 0.3125
- strengths: float32 [8], replicated, may hold values from 0.25 to 2
- regions: int32 [2, 8, 16], P('img', None, 'lon'), may hold values from 0 to 7
- control_kv: bfloat16 [320, 2560], replicated, may hold values from -1 to 1
- base_kv: bfloat16 [2, 128, 256, 2560], P('img', 'lat', 'lon'), may hold values from -12 to 12
- queries: bfloat16 [2, 32, 256, 1280], P('img', None, 'lon'), may hold values from -6 to 6
Outputs:
- features: bfloat16 [2, 128, 256, 320], P('img', 'lat', 'lon')
- attended: bfloat16 [2, 32, 256, 1280], P('img', 'lat', 'lon')
All inputs are finite; a program needn't handle non-finite values.
Results may differ from a plain program's by a relative error of at most 0.017.
Values may be sent and summed in bfloat16 or wider, within the bound.
A program may use at most 128 MiB of HBM per device.

v0:
```python
import jax
import jax.numpy as jnp
from jax import lax
from jax.sharding import PartitionSpec as P

HDIM = 64


NEG_START = -1e30


def padded(array, sides, width, wrap):
    for axis, dim in sides:
        size, length = (lax.axis_size(axis), array.shape[dim])
        up = [(i, (i + 1) % size) for i in range(size if wrap else size - 1)]
        down = [(j, i) for i, j in up]
        last = lax.slice_in_dim(array, length - width, length, axis=dim)
        first = lax.slice_in_dim(array, 0, width, axis=dim)
        before = lax.ppermute(last, axis, up)
        after = lax.ppermute(first, axis, down)
        array = jnp.concatenate([before, array, after], axis=dim)
    return array


def joined(value, axis, join):
    pieces = jax.tree.map(lambda part: lax.all_gather(part, axis), value)
    head = jax.tree.map(lambda part: part[0], pieces)
    tail = jax.tree.map(lambda part: part[1:], pieces)
    so_far, _ = lax.scan(lambda so_far, slab: (join(so_far, slab), None), head, tail)
    return so_far


def attend_block(softmax_state, both_queries, key_block):
    row_peak, row_total, numerator = softmax_state
    images, query_count, head_count, head_size = both_queries.shape
    key_width = head_count * head_size
    key_rows = key_block.shape[1]
    key_part = key_block[..., :key_width].reshape(images, key_rows, head_count, head_size)
    value_part = key_block[..., key_width:].reshape(images, key_rows, head_count, head_size)
    scores = jnp.einsum(
        "bqhe,bkhe->bqhk", both_queries, key_part, preferred_element_type=jnp.float32
    ) * head_size ** (-0.5)
    new_peak = jnp.maximum(row_peak, jnp.max(scores, axis=3))
    exp_scores = jnp.exp(scores - new_peak[..., None])
    fading = jnp.exp(row_peak - new_peak)
    row_total = row_total * fading + jnp.sum(exp_scores, axis=3)
    update = jnp.einsum(
        "bqhk,bkhe->bqhe",
        exp_scores.astype(jnp.bfloat16),
        value_part,
        preferred_element_type=jnp.float32,
    )
    numerator = (
        numerator.reshape(images, query_count, head_count, head_size) * fading[..., None] + update
    )
    return (new_peak, row_total, numerator.reshape(images, query_count, key_width))


def combine_states(former, latter):
    former_peak, former_total, former_sum = former
    latter_peak, latter_total, latter_sum = latter
    joint_peak = jnp.maximum(former_peak, latter_peak)
    former_fade = jnp.exp(former_peak - joint_peak)
    latter_fade = jnp.exp(latter_peak - joint_peak)
    split_shape = former_sum.shape[:2] + (former_peak.shape[2], -1)
    joint_sum = (
        former_sum.reshape(split_shape) * former_fade[..., None]
        + latter_sum.reshape(split_shape) * latter_fade[..., None]
    )
    return (
        joint_peak,
        former_total * former_fade + latter_total * latter_fade,
        joint_sum.reshape(former_sum.shape),
    )


def body(
    control, conv_weight, conv_bias, zero_weight, strengths, regions, control_kv, base_kv, queries
):
    images, lat_cells, lon_cells, channels = control.shape
    wrapped = padded(control, (("lon", 2),), 1, True)
    framed = padded(wrapped, (("lat", 1),), 1, False)
    taps = jnp.concatenate(
        [
            framed[:, row_tap : row_tap + lat_cells, col_tap : col_tap + lon_cells]
            for row_tap in range(3)
            for col_tap in range(3)
        ],
        axis=3,
    )
    convolved = jnp.dot(
        taps.reshape(-1, 9 * channels),
        conv_weight.reshape(9 * channels, channels),
        preferred_element_type=jnp.float32,
    )
    active = jax.nn.silu(convolved + conv_bias[None, :]).astype(jnp.bfloat16)
    branch = jnp.dot(active, zero_weight, preferred_element_type=jnp.float32).reshape(
        images, lat_cells, lon_cells, channels
    )
    row_global = lax.axis_index("lat") * lat_cells + jnp.arange(lat_cells)
    row_pick = (row_global[:, None] // 16 == jnp.arange(regions.shape[1])[None, :]).astype(
        jnp.float32
    )
    col_pick = (
        jnp.arange(lon_cells)[:, None] // 16 == jnp.arange(regions.shape[2])[None, :]
    ).astype(jnp.float32)
    cell_region = jnp.einsum("rR,bRC,cC->brc", row_pick, regions.astype(jnp.float32), col_pick)
    region_match = (
        cell_region[..., None] == jnp.arange(strengths.shape[0]).astype(jnp.float32)
    ).astype(jnp.float32)
    cell_strength = jnp.sum(region_match * strengths, axis=3)
    features = (control.astype(jnp.float32) + cell_strength[..., None] * branch).astype(
        jnp.bfloat16
    )
    head_width = queries.shape[3]
    head_count = head_width // HDIM
    kv_delta = jnp.dot(
        features.reshape(-1, channels), control_kv, preferred_element_type=jnp.float32
    )
    key_value = (
        base_kv.astype(jnp.float32) + kv_delta.reshape(images, lat_cells, lon_cells, 2 * head_width)
    ).astype(jnp.bfloat16)
    band_rows = queries.shape[1]
    query_count = band_rows * lon_cells
    own_queries = queries.reshape(images, query_count, head_count, HDIM)
    tile_keys = lat_cells * lon_cells
    flat_keys = lax.all_gather(key_value, "lon", axis=2, tiled=True).reshape(
        images, -1, 2 * head_width
    )
    tile_count = flat_keys.shape[1] // tile_keys
    group_size = max(
        (
            divisor
            for divisor in range(1, tile_count + 1)
            if tile_count % divisor == 0 and divisor * tile_keys <= max(512, tile_keys)
        )
    )

    def visit_block(turn_index, running):
        key_block = lax.dynamic_slice_in_dim(
            flat_keys, turn_index * group_size * tile_keys, group_size * tile_keys, 1
        )
        return attend_block(running, own_queries, key_block)

    softmax_state = lax.fori_loop(
        0,
        tile_count // group_size,
        visit_block,
        (
            jnp.full((images, query_count, head_count), NEG_START, jnp.float32),
            jnp.zeros((images, query_count, head_count), jnp.float32),
            jnp.zeros((images, query_count, head_width), jnp.float32),
        ),
    )
    row_peak, row_total, numerator = softmax_state
    share = band_rows // lax.axis_size("lat")
    row_peak, row_total, numerator = joined((row_peak, row_total, numerator), "lat", combine_states)
    band_sum = numerator.reshape(images, band_rows, lon_cells, head_count, HDIM)
    band_total = row_total.reshape(images, band_rows, lon_cells, head_count)
    my_sum = lax.dynamic_slice_in_dim(band_sum, lax.axis_index("lat") * share, share, 1)
    my_total = lax.dynamic_slice_in_dim(band_total, lax.axis_index("lat") * share, share, 1)
    attended = (
        (my_sum / my_total[..., None])
        .reshape(images, share, lon_cells, head_width)
        .astype(jnp.bfloat16)
    )
    return (features, attended)


def solution(mesh):
    in_specs = (
        P("img", "lat", "lon", None),
        P(),
        P(),
        P(),
        P(),
        P("img", None, "lon"),
        P(),
        P("img", "lat", "lon", None),
        P("img", None, "lon", None),
    )
    out_specs = (P("img", "lat", "lon", None), P("img", "lat", "lon", None))
    return jax.shard_map(body, mesh=mesh, in_specs=in_specs, out_specs=out_specs, check_vma=False)
```

profile of v0, /device:TPU:8, one launch (start us, length us, event | category | flops | bytes accessed | tf_op | source)
XLA Modules:
  0.0 936.1 jit_solution(14425703917397467285)
XLA Ops:
  49.2 264.3 %all-gather.6.cloned.1.call-done = bf16[1,16,256,2560]{3,2,1,0:T(8,128)(2,1)} async-done(((bf16[1,16,16,2560]{3,2,1,0:T(8,128)(2,1)}), bf16[1,16,256,2560]{3,2,1,0:T(8,128)(2,1)}) %all-gather.6.cloned.1.call-update) | async-done | bytes 20971536 | tf_op jit(solution)/shard_map/all_gather | solution.py:127
  315.3 286.0 %while.35 = (s32[]{:T(128)}, f32[1,512,20]{1,2,0:T(8,128)S(1)}, f32[1,512,20]{1,2,0:T(8,128)S(1)}, f32[1,512,1280]{1,2,0:T(8,128)}, bf16[1,4096,2560]{2,1,0:T(8,...) while((s32[]{:T(128)}, f32[1,512,20]{1,2,0:T(8,128)S(1)}, ...), condition=%wide.region_4.5_spmd.clone, body=%wide.region_1.4_spmd.clone.sunk | while | flops 1385492480 | bytes 83230904 | solution.py:145
  319.9 9.9 %bitcast_reduce_fusion.2 = (f32[512,20]{0,1:T(8,128)S(1)}, f32[20,512,512]{2,1,0:T(8,128)}) fusion(bf16[512,20,64]{0,2,1:T(8,128)(2,1)S(1)} %bitcast.156, bf16[1,512,20,64]{1,3,2,0:T(8,128)(2,1)} %get-tuple-element.454), kind=kOutput, calls=%fused_computation.13.clone.1 | convolution fusion | flops 681564160 | bytes 23633920 | tf_op jit(solution)/shard_map/while/body/eval_jaxpr/bqhe,bkhe->bqhk/dot_general | solution.py:40
  330.5 11.5 %bitcast_add_fusion.5 = f32[1,512,20,64]{1,3,2,0:T(8,128)} fusion(f32[1,512,20,64]{1,3,2,0:T(8,128)} %bitcast.158, bf16[512,20,64]{0,2,1:T(8,128)(2,1)S(1)} %bitcast.157, f32[20,512,512]{2,1,0:T(8,128)} %get-tuple-element.424, f32[512,20]{0,1:T(8,128)S(1)} %bitcast.160, f32[512,20]{0,1:T(8,128)S(1)} %get-tuple-element.426), kind=kOutput, calls=%fused_computation.21.clone.1 | convolution fusion | flops 688128000 | bytes 27607040 | tf_op jit(solution)/shard_map/while/body/eval_jaxpr/bqhk,bkhe->bqhe/dot_general | solution.py:47
  355.7 9.9 %bitcast_reduce_fusion.2 = (f32[512,20]{0,1:T(8,128)S(1)}, f32[20,512,512]{2,1,0:T(8,128)}) fusion(bf16[512,20,64]{0,2,1:T(8,128)(2,1)S(1)} %bitcast.156, bf16[1,512,20,64]{1,3,2,0:T(8,128)(2,1)} %get-tuple-element.454), kind=kOutput, calls=%fused_computation.13.clone.1 | convolution fusion | flops 681564160 | bytes 23633920 | tf_op jit(solution)/shard_map/while/body/eval_jaxpr/bqhe,bkhe->bqhk/dot_general | solution.py:40
  366.3 11.5 %bitcast_add_fusion.5 = f32[1,512,20,64]{1,3,2,0:T(8,128)} fusion(f32[1,512,20,64]{1,3,2,0:T(8,128)} %bitcast.158, bf16[512,20,64]{0,2,1:T(8,128)(2,1)S(1)} %bitcast.157, f32[20,512,512]{2,1,0:T(8,128)} %get-tuple-element.424, f32[512,20]{0,1:T(8,128)S(1)} %bitcast.160, f32[512,20]{0,1:T(8,128)S(1)} %get-tuple-element.426), kind=kOutput, calls=%fused_computation.21.clone.1 | convolution fusion | flops 688128000 | bytes 27607040 | tf_op jit(solution)/shard_map/while/body/eval_jaxpr/bqhk,bkhe->bqhe/dot_general | solution.py:47
  377.8 9.0 fusion.51
  391.4 9.9 %bitcast_reduce_fusion.2 = (f32[512,20]{0,1:T(8,128)S(1)}, f32[20,512,512]{2,1,0:T(8,128)}) fusion(bf16[512,20,64]{0,2,1:T(8,128)(2,1)S(1)} %bitcast.156, bf16[1,512,20,64]{1,3,2,0:T(8,128)(2,1)} %get-tuple-element.454), kind=kOutput, calls=%fused_computation.13.clone.1 | convolution fusion | flops 681564160 | bytes 23633920 | tf_op jit(solution)/shard_map/while/body/eval_jaxpr/bqhe,bkhe->bqhk/dot_general | solution.py:40
  402.0 11.5 %bitcast_add_fusion.5 = f32[1,512,20,64]{1,3,2,0:T(8,128)} fusion(f32[1,512,20,64]{1,3,2,0:T(8,128)} %bitcast.158, bf16[512,20,64]{0,2,1:T(8,128)(2,1)S(1)} %bitcast.157, f32[20,512,512]{2,1,0:T(8,128)} %get-tuple-element.424, f32[512,20]{0,1:T(8,128)S(1)} %bitcast.160, f32[512,20]{0,1:T(8,128)S(1)} %get-tuple-element.426), kind=kOutput, calls=%fused_computation.21.clone.1 | convolution fusion | flops 688128000 | bytes 27607040 | tf_op jit(solution)/shard_map/while/body/eval_jaxpr/bqhk,bkhe->bqhe/dot_general | solution.py:47
  427.2 9.9 %bitcast_reduce_fusion.2 = (f32[512,20]{0,1:T(8,128)S(1)}, f32[20,512,512]{2,1,0:T(8,128)}) fusion(bf16[512,20,64]{0,2,1:T(8,128)(2,1)S(1)} %bitcast.156, bf16[1,512,20,64]{1,3,2,0:T(8,128)(2,1)} %get-tuple-element.454), kind=kOutput, calls=%fused_computation.13.clone.1 | convolution fusion | flops 681564160 | bytes 23633920 | tf_op jit(solution)/shard_map/while/body/eval_jaxpr/bqhe,bkhe->bqhk/dot_general | solution.py:40
  437.8 11.5 %bitcast_add_fusion.5 = f32[1,512,20,64]{1,3,2,0:T(8,128)} fusion(f32[1,512,20,64]{1,3,2,0:T(8,128)} %bitcast.158, bf16[512,20,64]{0,2,1:T(8,128)(2,1)S(1)} %bitcast.157, f32[20,512,512]{2,1,0:T(8,128)} %get-tuple-element.424, f32[512,20]{0,1:T(8,128)S(1)} %bitcast.160, f32[512,20]{0,1:T(8,128)S(1)} %get-tuple-element.426), kind=kOutput, calls=%fused_computation.21.clone.1 | convolution fusion | flops 688128000 | bytes 27607040 | tf_op jit(solution)/shard_map/while/body/eval_jaxpr/bqhk,bkhe->bqhe/dot_general | solution.py:47
  462.9 9.9 %bitcast_reduce_fusion.2 = (f32[512,20]{0,1:T(8,128)S(1)}, f32[20,512,512]{2,1,0:T(8,128)}) fusion(bf16[512,20,64]{0,2,1:T(8,128)(2,1)S(1)} %bitcast.156, bf16[1,512,20,64]{1,3,2,0:T(8,128)(2,1)} %get-tuple-element.454), kind=kOutput, calls=%fused_computation.13.clone.1 | convolution fusion | flops 681564160 | bytes 23633920 | tf_op jit(solution)/shard_map/while/body/eval_jaxpr/bqhe,bkhe->bqhk/dot_general | solution.py:40
  473.5 11.5 %bitcast_add_fusion.5 = f32[1,512,20,64]{1,3,2,0:T(8,128)} fusion(f32[1,512,20,64]{1,3,2,0:T(8,128)} %bitcast.158, bf16[512,20,64]{0,2,1:T(8,128)(2,1)S(1)} %bitcast.157, f32[20,512,512]{2,1,0:T(8,128)} %get-tuple-element.424, f32[512,20]{0,1:T(8,128)S(1)} %bitcast.160, f32[512,20]{0,1:T(8,128)S(1)} %get-tuple-element.426), kind=kOutput, calls=%fused_computation.21.clone.1 | convolution fusion | flops 688128000 | bytes 27607040 | tf_op jit(solution)/shard_map/while/body/eval_jaxpr/bqhk,bkhe->bqhe/dot_general | solution.py:47
  498.7 9.9 %bitcast_reduce_fusion.2 = (f32[512,20]{0,1:T(8,128)S(1)}, f32[20,512,512]{2,1,0:T(8,128)}) fusion(bf16[512,20,64]{0,2,1:T(8,128)(2,1)S(1)} %bitcast.156, bf16[1,512,20,64]{1,3,2,0:T(8,128)(2,1)} %get-tuple-element.454), kind=kOutput, calls=%fused_computation.13.clone.1 | convolution fusion | flops 681564160 | bytes 23633920 | tf_op jit(solution)/shard_map/while/body/eval_jaxpr/bqhe,bkhe->bqhk/dot_general | solution.py:40
  509.3 11.5 %bitcast_add_fusion.5 = f32[1,512,20,64]{1,3,2,0:T(8,128)} fusion(f32[1,512,20,64]{1,3,2,0:T(8,128)} %bitcast.158, bf16[512,20,64]{0,2,1:T(8,128)(2,1)S(1)} %bitcast.157, f32[20,512,512]{2,1,0:T(8,128)} %get-tuple-element.424, f32[512,20]{0,1:T(8,128)S(1)} %bitcast.160, f32[512,20]{0,1:T(8,128)S(1)} %get-tuple-element.426), kind=kOutput, calls=%fused_computation.21.clone.1 | convolution fusion | flops 688128000 | bytes 27607040 | tf_op jit(solution)/shard_map/while/body/eval_jaxpr/bqhk,bkhe->bqhe/dot_general | solution.py:47
  534.4 9.9 %bitcast_reduce_fusion.2 = (f32[512,20]{0,1:T(8,128)S(1)}, f32[20,512,512]{2,1,0:T(8,128)}) fusion(bf16[512,20,64]{0,2,1:T(8,128)(2,1)S(1)} %bitcast.156, bf16[1,512,20,64]{1,3,2,0:T(8,128)(2,1)} %get-tuple-element.454), kind=kOutput, calls=%fused_computation.13.clone.1 | convolution fusion | flops 681564160 | bytes 23633920 | tf_op jit(solution)/shard_map/while/body/eval_jaxpr/bqhe,bkhe->bqhk/dot_general | solution.py:40
  545.0 11.5 %bitcast_add_fusion.5 = f32[1,512,20,64]{1,3,2,0:T(8,128)} fusion(f32[1,512,20,64]{1,3,2,0:T(8,128)} %bitcast.158, bf16[512,20,64]{0,2,1:T(8,128)(2,1)S(1)} %bitcast.157, f32[20,512,512]{2,1,0:T(8,128)} %get-tuple-element.424, f32[512,20]{0,1:T(8,128)S(1)} %bitcast.160, f32[512,20]{0,1:T(8,128)S(1)} %get-tuple-element.426), kind=kOutput, calls=%fused_computation.21.clone.1 | convolution fusion | flops 688128000 | bytes 27607040 | tf_op jit(solution)/shard_map/while/body/eval_jaxpr/bqhk,bkhe->bqhe/dot_general | solution.py:47
  570.2 9.9 %bitcast_reduce_fusion.2 = (f32[512,20]{0,1:T(8,128)S(1)}, f32[20,512,512]{2,1,0:T(8,128)}) fusion(bf16[512,20,64]{0,2,1:T(8,128)(2,1)S(1)} %bitcast.156, bf16[1,512,20,64]{1,3,2,0:T(8,128)(2,1)} %get-tuple-element.454), kind=kOutput, calls=%fused_computation.13.clone.1 | convolution fusion | flops 681564160 | bytes 23633920 | tf_op jit(solution)/shard_map/while/body/eval_jaxpr/bqhe,bkhe->bqhk/dot_general | solution.py:40
  580.8 11.5 %bitcast_add_fusion.5 = f32[1,512,20,64]{1,3,2,0:T(8,128)} fusion(f32[1,512,20,64]{1,3,2,0:T(8,128)} %bitcast.158, bf16[512,20,64]{0,2,1:T(8,128)(2,1)S(1)} %bitcast.157, f32[20,512,512]{2,1,0:T(8,128)} %get-tuple-element.424, f32[512,20]{0,1:T(8,128)S(1)} %bitcast.160, f32[512,20]{0,1:T(8,128)S(1)} %get-tuple-element.426), kind=kOutput, calls=%fused_computation.21.clone.1 | convolution fusion | flops 688128000 | bytes 27607040 | tf_op jit(solution)/shard_map/while/body/eval_jaxpr/bqhk,bkhe->bqhe/dot_general | solution.py:47
  604.6 28.8 %all-gather = f32[8,512,20]{1,2,0:T(8,128)S(1)} all-gather(f32[1,512,20]{1,2,0:T(8,128)S(1)} %get-tuple-element.196), channel_id=2, replica_groups=mesh['lon'=16,'lat'=8,'img'=2] {'lat'}, dimensions={0}, use_global_device_ids=true | all-gather | bytes 368640 | tf_op jit(solution)/shard_map/all_gather | solution.py:26
  633.4 30.0 %all-gather.1 = f32[8,512,20]{1,2,0:T(8,128)S(1)} all-gather(f32[1,512,20]{1,2,0:T(8,128)S(1)} %get-tuple-element.197), channel_id=3, replica_groups=mesh['lon'=16,'lat'=8,'img'=2] {'lat'}, dimensions={0}, use_global_device_ids=true | all-gather | bytes 368640 | tf_op jit(solution)/shard_map/all_gather | solution.py:26
  663.4 154.5 %all-gather.8.cloned.1.call-done = f32[8,512,1280]{2,1,0:T(8,128)} async-done(((f32[1,512,1280]{2,1,0:T(8,128)}), f32[8,512,1280]{2,1,0:T(8,128)}) %all-gather.8.cloned.1.call-update) | async-done | bytes 20971536 | tf_op jit(solution)/shard_map/all_gather | solution.py:26
  824.6 12.5 %slice_bitcast_fusion = f32[7,1,512,1280]{3,2,0,1:T(8,128)} fusion(f32[8,512,1280]{2,1,0:T(8,128)} %all-gather.8.cloned.1.call-done), kind=kLoop, calls=%fused_computation.32 | loop fusion | bytes 36700160 | tf_op jit(solution)/shard_map/slice | solution.py:28
  837.1 80.5 %while.34 = (s32[]{:T(128)}, f32[1,512,20]{1,2,0:T(8,128)S(1)}, f32[1,512,20]{1,2,0:T(8,128)S(1)}, f32[1,512,1280]{1,2,0:T(8,128)}, f32[7,1,512,20]{2,3,1,0:T(8,...) while((s32[]{:T(128)}, f32[1,512,20]{1,2,0:T(8,128)S(1)}, ...), condition=%wide.region_6.7_spmd, body=%wide.region_5.6_spmd.sunk | while | flops 2037762 | bytes 18964576 | solution.py:29
  (161 shorter events, 251.1 us)
Async XLA Ops:
  7.2 27.2 %copy-start = (bf16[3,3,320,320]{3,2,1,0:T(8,128)(2,1)S(1)}, bf16[3,3,320,320]{3,2,1,0:T(8,128)(2,1)}, u32[]{:S(2)}) copy-start(bf16[3,3,320,320]{3,2,1,0:T(8,128)(2,1)} %param.14) | copy-start | bytes 5529604
  7.2 23.6 %copy-start.3 = (bf16[1,16,16,320]{3,2,1,0:T(8,128)(2,1)S(1)}, bf16[1,16,16,320]{3,2,1,0:T(8,128)(2,1)}, u32[]{:S(2)}) copy-start(bf16[1,16,16,320]{3,2,1,0:T(8,128)(2,1)} %param.13) | copy-start | bytes 491524
  7.2 306.3 %all-gather.6.cloned.1.call-start = ((), (), s32[]{:S(2)}) async-start(), calls=%async_computation | async-start | bytes 22282240 | tf_op jit(solution)/shard_map/all_gather | solution.py:127
  8.4 10.2 %collective-permute-start = (bf16[1,16,1,320]{3,2,1,0:T(2,128)(2,1)S(1)}, bf16[1,16,1,320]{3,2,1,0:T(2,128)(2,1)S(1)}, u32[]{:S(2)}, u32[]{:S(2)}) collective-permute-start(bf16[1,16,1,320]{3,2,1,0:T(2,128)(2,1)S(1)} %get-tuple-element.322), channel_id=1, source_target_pairs={{0,16},{16,32},{32,48},{48,64},{64,80},{80,96},{96,112},{112,128},... | collective-permute-start | bytes 30728 | tf_op jit(solution)/shard_map/ppermute | solution.py:19
  10.4 8.2 collective-permute-start.1
  19.4 7.8 collective-permute-start.2
  22.9 5.7 collective-permute-start.3
  29.9 4.4 copy-start.7
  37.1 4.0 copy-start.6
  37.2 4.1 copy-start.5
  41.1 776.8 %all-gather.8.cloned.1.call-start = ((), (), s32[]{:S(2)}) async-start(), calls=%async_computation.1 | async-start | bytes 23592960 | tf_op jit(solution)/shard_map/all_gather | solution.py:26
  633.4 187.9 %copy-start.2 = (f32[8,512,20]{1,2,0:T(8,128)}, f32[8,512,20]{1,2,0:T(8,128)S(1)}, u32[]{:S(2)}) copy-start(f32[8,512,20]{1,2,0:T(8,128)S(1)} %all-gather) | copy-start | bytes 983044
  663.4 157.9 %copy-start.4 = (f32[8,512,20]{1,2,0:T(8,128)}, f32[8,512,20]{1,2,0:T(8,128)S(1)}, u32[]{:S(2)}) copy-start(f32[8,512,20]{1,2,0:T(8,128)S(1)} %all-gather.1) | copy-start | bytes 983044
  824.6 12.5 %slice-start = ((f32[8,512,20]{1,2,0:T(8,128)}), f32[1,512,20]{1,2,0:T(8,128)S(1)}, s32[]{:S(2)}) async-start(f32[8,512,20]{1,2,0:T(8,128)} %copy-done.2), calls=%async_computation.2 | async-start | bytes 98304 | tf_op jit(solution)/shard_map/slice | solution.py:27
  824.6 12.5 %slice-start.1 = ((f32[8,512,20]{1,2,0:T(8,128)}), f32[1,512,20]{1,2,0:T(8,128)S(1)}, s32[]{:S(2)}) async-start(f32[8,512,20]{1,2,0:T(8,128)} %copy-done.4), calls=%async_computation.3 | async-start | bytes 98304 | tf_op jit(solution)/shard_map/slice | solution.py:27
  920.9 8.4 copy-start.1
Sparse Core Ops, SparseCore 0:
  41.3 272.1 all-gather.5
  604.7 213.1 all-gather.7
where the time goes:
time: 942 us; the launch traced here: 936 us
  waiting for transfers between devices  420 us (45%)
  matrix products  179 us (19%)
  local copies, waits for them, and re-layouts  137 us (15%)
  other arithmetic  112 us (12%)
  blocking collectives  58.8 us (6%)
  starting transfers between devices  14.4 us (2%)
  between operations  14.2 us (2%)
    all_gather x1, waiting for transfers between devices, body(): lax.all_gather(key_value, 'lon', axis=2, tiled=True)  264 us
    all_gather x1, waiting for transfers between devices, joined(): pieces = jax.tree.map(lambda part: lax.all_gather(part, axis), value)  154 us
    dot_general x8, matrix products, attend_block(): jnp.einsum('bqhk,bkhe->bqhe', exp_scores.astype(jnp.bfloat16), value_part...  92 us
    dot_general x8, matrix products, attend_block(): jnp.einsum('bqhe,bkhe->bqhk', both_queries, key_part, preferred_element_t...  79.2 us
    reduce_sum x8, other arithmetic, attend_block(): row_total = row_total * fading + jnp.sum(exp_scores, axis=3)  71.9 us
    all_gather x2, blocking collectives, joined(): pieces = jax.tree.map(lambda part: lax.all_gather(part, axis), value)  58.8 us
    dynamic_slice x14, local copies, waits for them, and re-layouts, joined(): lax.scan(lambda so_far, slab: (join(so_far, slab), None), head, tail)  46.9 us
    add x7, other arithmetic, combine_states(): former_sum.reshape(split_shape) * former_fade[..., None]  33.1 us
  transfers between devices with their start and end apart: 6, of which 3 were waited for; matrix products, arithmetic and copies ran while one was open for 1% of the time, Pallas kernels for 0%

commit v1 on v0

v1 whole, which is shorter than its diff:
```python
import jax
import jax.numpy as jnp
from jax import lax
from jax.experimental import pallas as pl
from jax.experimental.pallas import tpu as pltpu
from jax.sharding import PartitionSpec as P

F32, BF16 = jnp.float32, jnp.bfloat16
MESH = pl.DeviceIdType.MESH
NX, NY, NZ = 4, 4, 8
LON, LAT = 16, 8
TOK = 256
C = 320
HD = 64
HEADS = 20
PER = HEADS // NY
WIDE = HEADS * HD
PAIRS = NX * NY // 2
PAY_ROWS = TOK
O_ROWS = HD + 16
FIRST_TILES = (0, 2, 5, 7)
OTHER_TILES = (1, 3, 4, 6, 8, 9)


def dot(a, b):
    return jnp.dot(a, b, preferred_element_type=F32)


def kernel(
    ctl, cw, bias, zw, strg, reg, wkv, base, qin,
    feat, att,
    hs, hr, xs, pay, kv, qt, qb, s0, s1, osend, orecv, ct, fo, fr,
    h_s, h_r, q_s, q_r, y_s, y_r, x_s, x_r, w_s, w_r, o_s, o_r, f_s, f_r,
):
    lon, lat = lax.axis_index("lon"), lax.axis_index("lat")
    xh, z = lon // NZ, lon % NZ
    xl, y = lat // NY, lat % NY
    x = xh * 2 + xl
    right, left = (x + 1) % NX, (x + 3) % NX

    def at(px, py, pz):
        return {"lon": (px // 2) * NZ + pz, "lat": (px % 2) * NY + py}

    def remote(src, dst, send, recv, where):
        return pltpu.make_async_remote_copy(
            src_ref=src, dst_ref=dst, send_sem=send, recv_sem=recv, device_id=where, device_id_type=MESH
        )

    west, east = (lon + LON - 1) % LON, (lon + 1) % LON
    north, south = (lat + LAT - 1) % LAT, (lat + 1) % LAT
    around = (
        (west, north), (west, lat), (west, south),
        (east, north), (east, lat), (east, south),
        (lon, north), (lon, south),
    )

    def halo(k):
        src = hs.at[0] if k < 3 else hs.at[1] if k < 6 else ctl.at[pl.ds(0 if k == 6 else TOK - 16, 16)]
        return remote(src, hr.at[k], h_s.at[k], h_r.at[k], {"lon": around[k][0], "lat": around[k][1]})

    def q_send(j, k):
        return remote(qt.at[y * PER + j], qb.at[j, z], q_s.at[j, k], q_r.at[j, k], at(x, y, (z + k) % NZ))

    def q_recv(j, k):
        src = (z + NZ - k) % NZ
        return remote(qb.at[j, src], qb.at[j, src], q_s.at[j, k], q_r.at[j, k], at(x, y, src))

    def y_send(j, k):
        to = (y + k) % NY
        return remote(pay.at[j, to], kv.at[j, x, y], y_s.at[j, k], y_r.at[j, k], at(x, to, z))

    def y_recv(j, k):
        src = (y + NY - k) % NY
        return remote(kv.at[j, x, src], kv.at[j, x, src], y_s.at[j, k], y_r.at[j, k], at(x, src, z))

    def x_send(j, k):
        to = right if k == 0 else left
        return remote(kv.at[j, x], kv.at[j, x], x_s.at[j, k], x_r.at[j, k], at(to, y, z))

    def x_recv(j, k):
        src = left if k == 0 else right
        return remote(kv.at[j, src], kv.at[j, src], x_s.at[j, k], x_r.at[j, k], at(src, y, z))

    def w_send(j, k):
        slab, to = (left, right) if k == 0 else (right, left)
        ref = kv.at[j, slab, pl.ds(2 * k, 2)]
        return remote(ref, ref, w_s.at[j, k], w_r.at[j, k], at(to, y, z))

    def w_recv(j, k):
        ref = kv.at[j, (x + 2) % NX, pl.ds(2 * k, 2)]
        return remote(ref, ref, w_s.at[j, k], w_r.at[j, k], at(left if k == 0 else right, y, z))

    def o_send(j, k):
        return remote(osend.at[j, k], orecv.at[j, k], o_s.at[j, k], o_r.at[j, k], at(x, y, (z + k) % NZ))

    def f_send(k):
        to = (y + k) % NY
        return remote(fo.at[to], fr.at[y], f_s.at[k], f_r.at[k], at(x, to, z))

    def f_recv(k):
        src = (y + NY - k) % NY
        return remote(fr.at[src], fr.at[src], f_s.at[k], f_r.at[k], at(x, src, z))

    barrier = pltpu.get_barrier_semaphore()
    partners = [at(right, y, z), at(left, y, z)]
    partners += [at(x, (y + k) % NY, z) for k in range(1, NY)]
    partners += [at(x, y, (z + k) % NZ) for k in range(1, NZ)]
    partners += [{"lon": a, "lat": b} for a, b in around]
    for who in partners:
        pl.semaphore_signal(barrier, inc=1, device_id=who, device_id_type=MESH)

    row16 = lax.broadcasted_iota(jnp.int32, (16, TOK), 0)
    col16 = lax.broadcasted_iota(jnp.int32, (16, TOK), 1)
    for side, off in ((0, 0), (1, 15)):
        pick = jnp.where(col16 == row16 * 16 + off, 1.0, 0.0).astype(BF16)
        hs[side] = dot(pick, ctl[...]).astype(BF16)
    pl.semaphore_wait(barrier, len(partners))
    for k in range(8):
        halo(k).start()

    for p in range(HEADS // 2):
        tile = qin[pl.ds(pl.multiple_of(xl * TOK, TOK), TOK), p * 128 : (p + 1) * 128].astype(F32)
        turned = (tile.T * (HD**-0.5)).astype(BF16)
        qt[2 * p] = turned[:HD]
        qt[2 * p + 1] = turned[HD:]

    def q_out(j, _):
        for k in (4, 3, 5, 2, 6, 1, 7):
            q_send(j, k).start()
        qb[j, z] = qt[y * PER + j]
        return 0

    lax.fori_loop(0, PER, q_out, 0)

    for k in range(8):
        halo(k).wait_recv()
    top = hr[7].astype(F32) * jnp.where(lat > 0, 1.0, 0.0)
    bottom = hr[6].astype(F32) * jnp.where(lat < LAT - 1, 1.0, 0.0)
    middle = jnp.concatenate([top, ctl[...].astype(F32), bottom], axis=0)
    tall = TOK + 32
    row = lax.broadcasted_iota(jnp.int32, (tall, 48), 0)
    pos = lax.broadcasted_iota(jnp.int32, (tall, 48), 1)
    first = jnp.where(lat > 0, 15, 16)
    last = jnp.where(lat < LAT - 1, 32, 31)
    wanted = (pos == row // 16 + 15) & (pos >= first) & (pos <= last)
    rows = lax.broadcasted_iota(jnp.int32, (tall, C), 0) % 16
    for tap, slots, edge, turn in ((0, (5, 4, 3), 0, 1), (2, (2, 1, 0), 15, tall - 1)):
        columns = jnp.concatenate([hr[s] for s in slots], axis=0)
        spread = dot(jnp.where(wanted & (row % 16 == edge), 1.0, 0.0).astype(BF16), columns)
        xs[tap] = jnp.where(rows == edge, spread, pltpu.roll(middle, turn, 0)).astype(BF16)
    xs[1] = middle.astype(BF16)
    total = jnp.zeros((TOK, C), F32)
    for dr in range(3):
        for dc in range(3):
            total += dot(xs[dc, 16 * dr : 16 * dr + TOK], cw[3 * dr + dc])
    total += bias[...]
    active = (total / (1.0 + jnp.exp(-total))).astype(BF16)
    branch = dot(active, zw[...])
    strength = strg[reg[lat]]
    features = (ctl[...].astype(F32) + strength * branch).astype(BF16)
    feat[...] = features

    low = lax.broadcasted_iota(jnp.int32, (128, 128), 1) < HD

    def project(p):
        def part(col):
            out = base[:, col : col + 128].astype(F32) + dot(feat[...], wkv[:, col : col + 128])
            return out.astype(BF16).astype(F32)

        keys, turned = part(p * 128), part(WIDE + p * 128).T
        a, b = keys[:128], keys[128:]
        packed = (jnp.where(low, a, pltpu.roll(b, HD, 1)), jnp.where(low, pltpu.roll(a, HD, 1), b))
        for half in range(2):
            g, j = divmod(2 * p + half, PER)
            pay[j, g, 0:128] = packed[half].astype(BF16)
            pay[j, g, 128:192] = turned[half * HD : (half + 1) * HD, :128].astype(BF16)
            pay[j, g, 192:256] = turned[half * HD : (half + 1) * HD, 128:].astype(BF16)

    def y_out(j):
        for k in (2, 1, 3):
            y_send(j, k).start()
        kv[j, x, y] = pay[j, y]

    for p in FIRST_TILES:
        project(p)
    y_out(0)
    for p in OTHER_TILES:
        project(p)
    lax.fori_loop(1, PER, lambda j, _: (y_out(j), 0)[1], 0)

    def spread_start(j):
        for k in range(1, NY):
            y_recv(j, k).wait_recv()
        for k in range(2):
            x_send(j, k).start()

    def spread_more(j):
        for k in range(2):
            x_recv(j, k).wait_recv()
        for k in range(2):
            w_send(j, k).start()

    def spread_end(j):
        for k in range(2):
            w_recv(j, k).wait_recv()
        for k in range(1, NZ):
            q_recv(j, k).wait_recv()

    nothing = jnp.zeros((HD, TOK), BF16)
    ones = jnp.ones((16, TOK), BF16)

    def weights_of(j, k):
        q = qb[j, (z + k) % NZ]
        return jnp.concatenate(
            [jnp.concatenate([q, nothing], axis=0), jnp.concatenate([nothing, q], axis=0)], axis=1
        )

    def score(j, w, p, scores, peak):
        keys = kv[j, p // 2, 2 * (p % 2) : 2 * (p % 2) + 2, 0:128].reshape(TOK, 128)
        s = dot(keys, w)
        for half in range(2):
            part = s[:, half * TOK : (half + 1) * TOK]
            scores[(2 * p + half) * TOK : (2 * p + half + 1) * TOK] = part
            peak = jnp.maximum(peak, part.reshape(TOK // 8, 8, TOK).max(0))
        return peak

    def gather(j, p, scores, peak, acc):
        for half in range(2):
            s = scores[(2 * p + half) * TOK : (2 * p + half + 1) * TOK]
            weights = jnp.exp(s - peak).astype(BF16)
            begin = 128 + half * HD
            v = jnp.concatenate(
                [kv[j, p // 2, 2 * (p % 2) + u, begin : begin + HD] for u in range(2)], axis=1
            )
            acc += dot(jnp.concatenate([v, ones], axis=0), weights)
        return acc

    low_peak = jnp.full((8, TOK), -jnp.inf, F32)

    def packed_result(acc, peak):
        sums = acc[HD : HD + 1]
        log_sum = peak + jnp.log(sums)
        hi = log_sum.astype(BF16).astype(F32)
        mid = (log_sum - hi).astype(BF16).astype(F32)
        lo = log_sum - hi - mid
        r = lax.broadcasted_iota(jnp.int32, (16, TOK), 0)
        stats = jnp.where(r == 0, hi, jnp.where(r == 1, mid, jnp.where(r == 2, lo, 0.0)))
        return jnp.concatenate([acc[:HD] * (1.0 / sums), stats], axis=0).astype(BF16)

    def both(j, nj, nk, ready, coming, peak):
        w = weights_of(nj, nk)
        next_peak, acc = low_peak, jnp.zeros((O_ROWS, TOK), F32)
        for p in range(PAIRS):
            next_peak = score(nj, w, p, coming, next_peak)
            acc = gather(j, p, ready, peak, acc)
        return packed_result(acc, peak), next_peak.max(0, keepdims=True)

    def join(j):
        parts, logs = [], []
        for k in range(NZ):
            if k > 0:
                o_send(j, k).wait_recv()
            logs.append(orecv[j, k, HD : HD + 16].astype(F32)[0:3].sum(0, keepdims=True))
        top_log = logs[0]
        for other in logs[1:]:
            top_log = jnp.maximum(top_log, other)
        out, whole = jnp.zeros((HD, TOK), F32), jnp.zeros((1, TOK), F32)
        for k in range(NZ):
            share = jnp.exp(logs[k] - top_log)
            whole += share
            out += orecv[j, k, 0:HD].astype(F32) * share
        ct[j] = out * (1.0 / whole)

    spread_start(0)
    spread_more(0)
    spread_end(0)
    w = weights_of(0, 4)
    peak = low_peak
    for p in range(PAIRS):
        peak = score(0, w, p, s0, peak)
    peak = peak.max(0, keepdims=True)

    def step(n, peak):
        j, i = n // 4, n % 4
        more = j < PER - 1

        @pl.when((i == 0) & more)
        def _():
            spread_start(j + 1)

        @pl.when((i == 2) & more)
        def _():
            spread_more(j + 1)

        @pl.when((i == 1) & (j > 0))
        def _():
            join(j - 1)

        result, peak = both(j, j, 3 - i, s0, s1, peak)
        osend[j, 4 + i] = result
        o_send(j, 4 + i).start()

        @pl.when((i == 3) & more)
        def _():
            spread_end(j + 1)

        nj = jnp.where((i == 3) & more, j + 1, j)
        nk = jnp.where(i == 3, 4, 5 + i)
        result, peak = both(j, nj, nk, s1, s0, peak)

        @pl.when(i < 3)
        def _():
            osend[j, 3 - i] = result
            o_send(j, 3 - i).start()

        @pl.when(i == 3)
        def _():
            orecv[j, 0] = result

        return peak

    lax.fori_loop(0, 4 * PER, step, peak)
    join(PER - 1)

    for t in range(3):
        if t < 2:
            turned = jnp.concatenate([ct[2 * t], ct[2 * t + 1]], axis=0).T
        else:
            turned = jnp.concatenate([ct[4], jnp.zeros((HD, TOK), F32)], axis=0).T
        for g in range(NY):
            fo[g, :, t * 128 : (t + 1) * 128] = turned[g * 64 : (g + 1) * 64].astype(BF16)
    for k in (2, 1, 3):
        f_send(k).start()
    fr[y] = fo[y]
    for k in range(1, NY):
        f_recv(k).wait_recv()
    att[...] = jnp.concatenate([fr[g][:, :C].astype(F32) for g in range(NY)], axis=1).astype(BF16)

    for k in range(8):
        halo(k).wait_send()

    def drain(j, _):
        for k in range(1, NZ):
            q_send(j, k).wait_send()
            o_send(j, k).wait_send()
        for k in range(1, NY):
            y_send(j, k).wait_send()
        for k in range(2):
            x_send(j, k).wait_send()
            w_send(j, k).wait_send()
        return 0

    lax.fori_loop(0, PER, drain, 0)
    for k in range(1, NY):
        f_send(k).wait_send()


def body(control, conv_weight, conv_bias, zero_weight, strengths, regions, control_kv, base_kv, queries):
    vmem = pl.BlockSpec(memory_space=pltpu.VMEM)
    smem = pl.BlockSpec(memory_space=pltpu.SMEM)
    dma = pltpu.SemaphoreType.DMA
    features, attended = pl.pallas_call(
        kernel,
        out_shape=[
            jax.ShapeDtypeStruct((TOK, C), BF16),
            jax.ShapeDtypeStruct((64, WIDE), BF16),
        ],
        in_specs=[vmem, vmem, vmem, vmem, smem, smem, vmem, vmem, vmem],
        out_specs=[vmem, vmem],
        scratch_shapes=[
            pltpu.VMEM((2, 16, C), BF16),
            pltpu.VMEM((8, 16, C), BF16),
            pltpu.VMEM((3, TOK + 32, C), BF16),
            pltpu.VMEM((PER, NY, PAY_ROWS, 128), BF16),
            pltpu.VMEM((PER, NX, NY, PAY_ROWS, 128), BF16),
            pltpu.VMEM((HEADS, HD, TOK), BF16),
            pltpu.VMEM((PER, NZ, HD, TOK), BF16),
            pltpu.VMEM((NX * NY * TOK, TOK), F32),
            pltpu.VMEM((NX * NY * TOK, TOK), F32),
            pltpu.VMEM((PER, NZ, O_ROWS, TOK), BF16),
            pltpu.VMEM((PER, NZ, O_ROWS, TOK), BF16),
            pltpu.VMEM((PER, HD, TOK), F32),
            pltpu.VMEM((NY, 64, 384), BF16),
            pltpu.VMEM((NY, 64, 384), BF16),
            dma((8,)), dma((8,)),
            dma((PER, NZ)), dma((PER, NZ)),
            dma((PER, NY)), dma((PER, NY)),
            dma((PER, 2)), dma((PER, 2)),
            dma((PER, 2)), dma((PER, 2)),
            dma((PER, NZ)), dma((PER, NZ)),
            dma((NY,)), dma((NY,)),
        ],
        compiler_params=pltpu.CompilerParams(
            collective_id=0, has_side_effects=True, vmem_limit_bytes=48 * 2**20
        ),
    )(
        control.reshape(TOK, C),
        conv_weight.reshape(9, C, C),
        conv_bias.reshape(1, C),
        zero_weight,
        strengths,
        regions.reshape(-1),
        control_kv,
        base_kv.reshape(TOK, 2 * WIDE),
        queries.reshape(2 * TOK, WIDE),
    )
    return features.reshape(1, 16, 16, C), attended.reshape(1, 4, 16, WIDE)


def solution(mesh):
    in_specs = (
        P("img", "lat", "lon", None),
        P(),
        P(),
        P(),
        P(),
        P("img", None, "lon"),
        P(),
        P("img", "lat", "lon", None),
        P("img", None, "lon", None),
    )
    out_specs = (P("img", "lat", "lon", None), P("img", "lat", "lon", None))
    return jax.shard_map(body, mesh=mesh, in_specs=in_specs, out_specs=out_specs, check_vma=False)
```

time: 942 us -> 119 us (0.13)
  waiting for transfers between devices: 420 us -> 0 us
  matrix products: 179 us -> 0 us
  local copies, waits for them, and re-layouts: 137 us -> 9.27 us
  other arithmetic: 112 us -> 0 us
  Pallas kernels: 0 us -> 108 us
  blocking collectives: 58.8 us -> 0 us
  starting transfers between devices: 14.4 us -> 0 us
  between operations: 14.2 us -> 0.65 us
    all_gather x2 -> x0, waiting for transfers between devices: 419 us -> none  [the longest x1 264 us: body(): lax.all_gather(key_value, 'lon', axis=2, tiled=True)]
    dot_general x19 -> x0, matrix products: 179 us -> none  [the longest x8 92 us: attend_block(): jnp.einsum('bqhk,bkhe->bqhe', exp_scores.astype(jnp.bfloat16), value_part...]
    pallas_call x0 -> x1, Pallas kernels: none -> 108 us  [body(): pl.pallas_call(kernel, out_shape=[jax.ShapeDtypeStruct((TOK, C), BF16), j...]
    reduce_sum x9 -> x0, other arithmetic: 72.6 us -> none  [the longest x8 71.9 us: attend_block(): row_total = row_total * fading + jnp.sum(exp_scores, axis=3)]
    all_gather x2 -> x0, blocking collectives: 58.8 us -> none  [joined(): pieces = jax.tree.map(lambda part: lax.all_gather(part, axis), value)]
    dynamic_slice x16 -> x0, local copies, waits for them, and re-layouts: 47 us -> none  [the longest x14 46.9 us: joined(): lax.scan(lambda so_far, slab: (join(so_far, slab), None), head, tail)]
    slice x16 -> x0, local copies, waits for them, and re-layouts: 41.9 us -> none  [the longest x8 23.9 us: attend_block(): key_block[..., key_width:].reshape(images, key_rows, head_count, head_size)]
    add x15 -> x0, other arithmetic: 33.3 us -> none  [the longest x7 33.1 us: combine_states(): former_sum.reshape(split_shape) * former_fade[..., None]]
  transfers between devices with their start and end apart: 6 -> 0, of which waited for: 3 -> 0; matrix products, arithmetic and copies ran while one was open for 1% -> 0% of each run, Pallas kernels for 0% -> 0%
where the time goes in v1:
time: 119 us; the launch traced here: 118 us
  Pallas kernels  108 us (91%)
  local copies, waits for them, and re-layouts  9.27 us (8%)
    pallas_call x1, Pallas kernels, body(): pl.pallas_call(kernel, out_shape=[jax.ShapeDtypeStruct((TOK, C), BF16), j...  108 us
    unnamed x16, local copies, waits for them, and re-layouts  8.59 us

profile of v1, /device:TPU:8, one launch (start us, length us, event | category | flops | bytes accessed | tf_op | source)
XLA Modules:
  0.0 118.3 jit_solution(3899225342527128695)
XLA Ops:
  0.6 0.7 reshape.30.bias
  1.3 0.0 copy-start
  1.3 1.4 %copy-done = bf16[320,2560]{1,0:T(8,128)(2,1)S(1)} copy-done((bf16[320,2560]{1,0:T(8,128)(2,1)S(1)}, bf16[320,2560]{1,0:T(8,128)(2,1)}, u32[]{:S(2)}) %copy-start) | copy-done | bytes 1638424
  2.7 0.0 copy-start.1
  2.7 1.3 %copy-done.1 = bf16[1,16,16,2560]{3,2,1,0:T(8,128)(2,1)S(1)} copy-done((bf16[1,16,16,2560]{3,2,1,0:T(8,128)(2,1)S(1)}, bf16[1,16,16,2560]{3,2,1,0:T(8,128)(2,1)}, u32[]{:S(2)}) %copy-start.1) | copy-done | bytes 1310744
  4.1 0.0 copy-start.2
  4.1 1.3 %copy-done.2 = bf16[1,32,16,1280]{3,2,1,0:T(8,128)(2,1)S(1)} copy-done((bf16[1,32,16,1280]{3,2,1,0:T(8,128)(2,1)S(1)}, bf16[1,32,16,1280]{3,2,1,0:T(8,128)(2,1)}, u32[]{:S(2)}) %copy-start.2) | copy-done | bytes 1310744
  5.4 0.0 copy-start.3
  5.4 0.9 copy-done.3
  6.3 0.0 copy-start.4
  6.3 0.9 copy-done.4
  7.3 0.0 copy-start.5
  7.3 0.7 copy-done.5
  7.9 0.0 copy-start.6
  7.9 0.7 copy-done.6
  8.6 108.4 %shard_map.104 = (bf16[256,320]{1,0:T(8,128)(2,1)S(1)}, bf16[64,1280]{1,0:T(8,128)(2,1)S(1)}) custom-call(bf16[256,320]{1,0:T(8,128)(2,1)S(1)} %bitcast.10, bf16[9,320,320]{2,1,0:T(8,128)(2,1)} %bitcast.13, f32[1,320]{1,0:T(1,128)S(1)} %reshape.30.bias, bf16[320,320]{1,0:T(8,128)(2,1)S(1)} %copy-done.3, f32[8]{0:T(128)S(1)} %copy-done.5, s32[8]{0:T(128)S(1)} %bitcast.12, ...), custom_call_target="tpu_custom_call" | custom-call | tf_op jit(solution)/shard_map/pallas_call | solution.py:362
  117.0 0.7 copy.13
  117.7 0.7 copy.14
Async XLA Ops:
  1.3 1.4 %copy-start = (bf16[320,2560]{1,0:T(8,128)(2,1)S(1)}, bf16[320,2560]{1,0:T(8,128)(2,1)}, u32[]{:S(2)}) copy-start(bf16[320,2560]{1,0:T(8,128)(2,1)} %wkv.1) | copy-start | bytes 4915204
  2.7 1.3 %copy-start.1 = (bf16[1,16,16,2560]{3,2,1,0:T(8,128)(2,1)S(1)}, bf16[1,16,16,2560]{3,2,1,0:T(8,128)(2,1)}, u32[]{:S(2)}) copy-start(bf16[1,16,16,2560]{3,2,1,0:T(8,128)(2,1)} %param.16) | copy-start | bytes 3932164
  4.1 1.3 %copy-start.2 = (bf16[1,32,16,1280]{3,2,1,0:T(8,128)(2,1)S(1)}, bf16[1,32,16,1280]{3,2,1,0:T(8,128)(2,1)}, u32[]{:S(2)}) copy-start(bf16[1,32,16,1280]{3,2,1,0:T(8,128)(2,1)} %param.17) | copy-start | bytes 3932164
  5.4 0.9 copy-start.3
  6.3 0.9 copy-start.4
  7.3 0.7 copy-start.5
  7.9 0.7 copy-start.6

commit v2 on v1

--- a/solution.py
+++ b/solution.py
@@ -27,10 +27,11 @@
 
 
 def kernel(
+    ctl_h, cw_h, bias_h, zw_h, strg_h, reg_h, wkv_h, base_h, qin_h,
+    feat, att,
     ctl, cw, bias, zw, strg, reg, wkv, base, qin,
-    feat, att,
     hs, hr, xs, pay, kv, qt, qb, s0, s1, osend, orecv, ct, fo, fr,
-    h_s, h_r, q_s, q_r, y_s, y_r, x_s, x_r, w_s, w_r, o_s, o_r, f_s, f_r,
+    in_s, h_s, h_r, q_s, q_r, y_s, y_r, x_s, x_r, w_s, w_r, o_s, o_r, f_s, f_r,
 ):
     lon, lat = lax.axis_index("lon"), lax.axis_index("lat")
     xh, z = lon // NZ, lon % NZ
@@ -58,12 +59,28 @@
         src = hs.at[0] if k < 3 else hs.at[1] if k < 6 else ctl.at[pl.ds(0 if k == 6 else TOK - 16, 16)]
         return remote(src, hr.at[k], h_s.at[k], h_r.at[k], {"lon": around[k][0], "lat": around[k][1]})
 
-    def q_send(j, k):
-        return remote(qt.at[y * PER + j], qb.at[j, z], q_s.at[j, k], q_r.at[j, k], at(x, y, (z + k) % NZ))
-
-    def q_recv(j, k):
-        src = (z + NZ - k) % NZ
-        return remote(qb.at[j, src], qb.at[j, src], q_s.at[j, k], q_r.at[j, k], at(x, y, src))
+    def q_part(step, k):
+        tile = (z + NZ - step) % NZ if k == 0 else (z + step) % NZ
+        if step < 3:
+            return qb.at[tile]
+        return qb.at[tile, pl.ds(0, 2)] if k == 0 else qb.at[tile, pl.ds(2, 3)]
+
+    def q_send(step, k):
+        ref = q_part(step, k)
+        to = (z + 1) % NZ if k == 0 else (z + NZ - 1) % NZ
+        return remote(ref, ref, q_s.at[step, k], q_r.at[step, k], at(x, y, to))
+
+    def q_recv(step, k):
+        tile = (z + NZ - step - 1) % NZ if k == 0 else (z + step + 1) % NZ
+        ref = qb.at[tile] if step < 3 else qb.at[tile, pl.ds(0, 2)] if k == 0 else qb.at[tile, pl.ds(2, 3)]
+        src = (z + NZ - 1) % NZ if k == 0 else (z + 1) % NZ
+        return remote(ref, ref, q_s.at[step, k], q_r.at[step, k], at(x, y, src))
+
+    def q_step(step):
+        for k in range(2):
+            if step > 0:
+                q_recv(step - 1, k).wait_recv()
+            q_send(step, k).start()
 
     def y_send(j, k):
         to = (y + k) % NY
@@ -73,13 +90,15 @@
         src = (y + NY - k) % NY
         return remote(kv.at[j, x, src], kv.at[j, x, src], y_s.at[j, k], y_r.at[j, k], at(x, src, z))
 
-    def x_send(j, k):
+    def x_send(j, k, part):
         to = right if k == 0 else left
-        return remote(kv.at[j, x], kv.at[j, x], x_s.at[j, k], x_r.at[j, k], at(to, y, z))
-
-    def x_recv(j, k):
+        ref = kv.at[j, x, pl.ds(2 * (k ^ part), 2)]
+        return remote(ref, ref, x_s.at[j, k, part], x_r.at[j, k, part], at(to, y, z))
+
+    def x_recv(j, k, part):
         src = left if k == 0 else right
-        return remote(kv.at[j, src], kv.at[j, src], x_s.at[j, k], x_r.at[j, k], at(src, y, z))
+        ref = kv.at[j, src, pl.ds(2 * (k ^ part), 2)]
+        return remote(ref, ref, x_s.at[j, k, part], x_r.at[j, k, part], at(src, y, z))
 
     def w_send(j, k):
         slab, to = (left, right) if k == 0 else (right, left)
@@ -100,6 +119,17 @@
     def f_recv(k):
         src = (y + NY - k) % NY
         return remote(fr.at[src], fr.at[src], f_s.at[k], f_r.at[k], at(x, src, z))
+
+    first_tile = (y * PER) // 2
+    rows_q = pl.ds(pl.multiple_of(xl * TOK, TOK), TOK)
+    lanes_q = pl.ds(pl.multiple_of(first_tile * 128, 128), 384)
+    pairs_in = (
+        (ctl_h, ctl), (qin_h.at[rows_q, lanes_q], qin), (cw_h, cw), (bias_h, bias), (zw_h, zw),
+        (strg_h, strg), (reg_h, reg), (base_h, base), (wkv_h, wkv),
+    )
+    fetch = [pltpu.make_async_copy(a, b, in_s.at[n]) for n, (a, b) in enumerate(pairs_in)]
+    for copy in fetch:
+        copy.start()
 
     barrier = pltpu.get_barrier_semaphore()
     partners = [at(right, y, z), at(left, y, z)]
@@ -109,28 +139,25 @@
     for who in partners:
         pl.semaphore_signal(barrier, inc=1, device_id=who, device_id_type=MESH)
 
+    fetch[0].wait()
     row16 = lax.broadcasted_iota(jnp.int32, (16, TOK), 0)
     col16 = lax.broadcasted_iota(jnp.int32, (16, TOK), 1)
     for side, off in ((0, 0), (1, 15)):
         pick = jnp.where(col16 == row16 * 16 + off, 1.0, 0.0).astype(BF16)
         hs[side] = dot(pick, ctl[...]).astype(BF16)
+
+    fetch[1].wait()
+    for t in range(3):
+        turned = (qin[:, t * 128 : (t + 1) * 128].astype(F32).T * (HD**-0.5)).astype(BF16)
+        qt[2 * t] = turned[:HD]
+        qt[2 * t + 1] = turned[HD:]
+    for j in range(PER):
+        qb[z, j] = qt[(y * PER) % 2 + j]
+
     pl.semaphore_wait(barrier, len(partners))
     for k in range(8):
         halo(k).start()
-
-    for p in range(HEADS // 2):
-        tile = qin[pl.ds(pl.multiple_of(xl * TOK, TOK), TOK), p * 128 : (p + 1) * 128].astype(F32)
-        turned = (tile.T * (HD**-0.5)).astype(BF16)
-        qt[2 * p] = turned[:HD]
-        qt[2 * p + 1] = turned[HD:]
-
-    def q_out(j, _):
-        for k in (4, 3, 5, 2, 6, 1, 7):
-            q_send(j, k).start()
-        qb[j, z] = qt[y * PER + j]
-        return 0
-
-    lax.fori_loop(0, PER, q_out, 0)
+    q_step(0)
 
     for k in range(8):
         halo(k).wait_recv()
@@ -149,16 +176,19 @@
         spread = dot(jnp.where(wanted & (row % 16 == edge), 1.0, 0.0).astype(BF16), columns)
         xs[tap] = jnp.where(rows == edge, spread, pltpu.roll(middle, turn, 0)).astype(BF16)
     xs[1] = middle.astype(BF16)
+    for n in (2, 3, 4, 5, 6):
+        fetch[n].wait()
     total = jnp.zeros((TOK, C), F32)
     for dr in range(3):
         for dc in range(3):
             total += dot(xs[dc, 16 * dr : 16 * dr + TOK], cw[3 * dr + dc])
-    total += bias[...]
+    total += bias[...].reshape(1, C)
     active = (total / (1.0 + jnp.exp(-total))).astype(BF16)
     branch = dot(active, zw[...])
     strength = strg[reg[lat]]
     features = (ctl[...].astype(F32) + strength * branch).astype(BF16)
     feat[...] = features
+    q_step(1)
 
     low = lax.broadcasted_iota(jnp.int32, (128, 128), 1) < HD
 
@@ -181,36 +211,37 @@
             y_send(j, k).start()
         kv[j, x, y] = pay[j, y]
 
+    fetch[7].wait()
+    fetch[8].wait()
     for p in FIRST_TILES:
         project(p)
     y_out(0)
     for p in OTHER_TILES:
         project(p)
-    lax.fori_loop(1, PER, lambda j, _: (y_out(j), 0)[1], 0)
+    q_step(2)
 
     def spread_start(j):
         for k in range(1, NY):
             y_recv(j, k).wait_recv()
-        for k in range(2):
-            x_send(j, k).start()
+        for part in range(2):
+            for k in range(2):
+                x_send(j, k, part).start()
 
     def spread_more(j):
         for k in range(2):
-            x_recv(j, k).wait_recv()
-        for k in range(2):
+            x_recv(j, k, 0).wait_recv()
             w_send(j, k).start()
 
     def spread_end(j):
         for k in range(2):
+            x_recv(j, k, 1).wait_recv()
             w_recv(j, k).wait_recv()
-        for k in range(1, NZ):
-            q_recv(j, k).wait_recv()
 
     nothing = jnp.zeros((HD, TOK), BF16)
     ones = jnp.ones((16, TOK), BF16)
 
     def weights_of(j, k):
-        q = qb[j, (z + k) % NZ]
+        q = qb[(z + k) % NZ, j]
         return jnp.concatenate(
             [jnp.concatenate([q, nothing], axis=0), jnp.concatenate([nothing, q], axis=0)], axis=1
         )
@@ -272,8 +303,13 @@
         ct[j] = out * (1.0 / whole)
 
     spread_start(0)
+    lax.fori_loop(1, PER, lambda j, _: (y_out(j), 0)[1], 0)
     spread_more(0)
+    spread_start(1)
+    q_step(3)
     spread_end(0)
+    for k in range(2):
+        q_recv(3, k).wait_recv()
     w = weights_of(0, 4)
     peak = low_peak
     for p in range(PAIRS):
@@ -284,15 +320,15 @@
         j, i = n // 4, n % 4
         more = j < PER - 1
 
-        @pl.when((i == 0) & more)
-        def _():
-            spread_start(j + 1)
-
-        @pl.when((i == 2) & more)
+        @pl.when((i == 1) & more)
         def _():
             spread_more(j + 1)
 
-        @pl.when((i == 1) & (j > 0))
+        @pl.when((i == 1) & (j < PER - 2))
+        def _():
+            spread_start(j + 2)
+
+        @pl.when((i == 2) & (j > 0))
         def _():
             join(j - 1)
 
@@ -339,14 +375,18 @@
     for k in range(8):
         halo(k).wait_send()
 
+    for step in range(4):
+        for k in range(2):
+            q_send(step, k).wait_send()
+
     def drain(j, _):
         for k in range(1, NZ):
-            q_send(j, k).wait_send()
             o_send(j, k).wait_send()
         for k in range(1, NY):
             y_send(j, k).wait_send()
         for k in range(2):
-            x_send(j, k).wait_send()
+            x_send(j, k, 0).wait_send()
+            x_send(j, k, 1).wait_send()
             w_send(j, k).wait_send()
         return 0
 
@@ -357,7 +397,7 @@
 
 def body(control, conv_weight, conv_bias, zero_weight, strengths, regions, control_kv, base_kv, queries):
     vmem = pl.BlockSpec(memory_space=pltpu.VMEM)
-    smem = pl.BlockSpec(memory_space=pltpu.SMEM)
+    hbm = pl.BlockSpec(memory_space=pltpu.HBM)
     dma = pltpu.SemaphoreType.DMA
     features, attended = pl.pallas_call(
         kernel,
@@ -365,16 +405,25 @@
             jax.ShapeDtypeStruct((TOK, C), BF16),
             jax.ShapeDtypeStruct((64, WIDE), BF16),
         ],
-        in_specs=[vmem, vmem, vmem, vmem, smem, smem, vmem, vmem, vmem],
+        in_specs=[hbm] * 9,
         out_specs=[vmem, vmem],
         scratch_shapes=[
+            pltpu.VMEM((TOK, C), BF16),
+            pltpu.VMEM((9, C, C), BF16),
+            pltpu.VMEM((C,), F32),
+            pltpu.VMEM((C, C), BF16),
+            pltpu.SMEM((8,), F32),
+            pltpu.SMEM((8,), jnp.int32),
+            pltpu.VMEM((C, 2 * WIDE), BF16),
+            pltpu.VMEM((TOK, 2 * WIDE), BF16),
+            pltpu.VMEM((TOK, 384), BF16),
             pltpu.VMEM((2, 16, C), BF16),
             pltpu.VMEM((8, 16, C), BF16),
             pltpu.VMEM((3, TOK + 32, C), BF16),
             pltpu.VMEM((PER, NY, PAY_ROWS, 128), BF16),
             pltpu.VMEM((PER, NX, NY, PAY_ROWS, 128), BF16),
-            pltpu.VMEM((HEADS, HD, TOK), BF16),
-            pltpu.VMEM((PER, NZ, HD, TOK), BF16),
+            pltpu.VMEM((6, HD, TOK), BF16),
+            pltpu.VMEM((NZ, PER, HD, TOK), BF16),
             pltpu.VMEM((NX * NY * TOK, TOK), F32),
             pltpu.VMEM((NX * NY * TOK, TOK), F32),
             pltpu.VMEM((PER, NZ, O_ROWS, TOK), BF16),
@@ -382,21 +431,22 @@
             pltpu.VMEM((PER, HD, TOK), F32),
             pltpu.VMEM((NY, 64, 384), BF16),
             pltpu.VMEM((NY, 64, 384), BF16),
+            dma((9,)),
             dma((8,)), dma((8,)),
-            dma((PER, NZ)), dma((PER, NZ)),
+            dma((4, 2)), dma((4, 2)),
             dma((PER, NY)), dma((PER, NY)),
-            dma((PER, 2)), dma((PER, 2)),
+            dma((PER, 2, 2)), dma((PER, 2, 2)),
             dma((PER, 2)), dma((PER, 2)),
             dma((PER, NZ)), dma((PER, NZ)),
             dma((NY,)), dma((NY,)),
         ],
         compiler_params=pltpu.CompilerParams(
-            collective_id=0, has_side_effects=True, vmem_limit_bytes=48 * 2**20
+            collective_id=0, has_side_effects=True, vmem_limit_bytes=63 * 2**20
         ),
     )(
         control.reshape(TOK, C),
         conv_weight.reshape(9, C, C),
-        conv_bias.reshape(1, C),
+        conv_bias,
         zero_weight,
         strengths,
         regions.reshape(-1),

time: 119 us -> 91.6 us (0.77)
  Pallas kernels: 108 us -> 87.6 us
  local copies, waits for them, and re-layouts: 9.27 us -> 3.22 us
    pallas_call x1, Pallas kernels: 108 us -> 87.6 us  [body(): pl.pallas_call(kernel, out_shape=[jax.ShapeDtypeStruct((TOK, C), BF16), j...]
    unnamed x16 -> x2, local copies, waits for them, and re-layouts: 8.59 us -> 3.22 us
where the time goes in v2:
time: 91.6 us; the launch traced here: 91.5 us
  Pallas kernels  87.6 us (96%)
  local copies, waits for them, and re-layouts  3.22 us (4%)
    pallas_call x1, Pallas kernels, body(): pl.pallas_call(kernel, out_shape=[jax.ShapeDtypeStruct((TOK, C), BF16), j...  87.6 us
    unnamed x2, local copies, waits for them, and re-layouts  3.22 us

profile of v2, /device:TPU:8, one launch (start us, length us, event | category | flops | bytes accessed | tf_op | source)
XLA Modules:
  0.0 91.5 jit_solution(2786260395965832144)
XLA Ops:
  0.6 87.6 %shard_map.104 = (bf16[256,320]{1,0:T(8,128)(2,1)}, bf16[64,1280]{1,0:T(8,128)(2,1)}) custom-call(bf16[256,320]{1,0:T(8,128)(2,1)} %bitcast.10, bf16[9,320,320]{2,1,0:T(8,128)(2,1)} %bitcast.7, f32[320]{0:T(512)} %bias_h.1, bf16[320,320]{1,0:T(8,128)(2,1)} %zw_h.1, f32[8]{0:T(128)} %strg_h.1, s32[8]{0:T(128)} %bitcast.13, bf16[320,2560]{1,0:T(8,128)(2,1)} %wkv_h.1, ...), custom_call_target="tpu_custom_call" | custom-call | tf_op jit(solution)/shard_map/pallas_call | solution.py:402
  88.3 1.6 %copy.13 = bf16[1,16,16,320]{3,2,1,0:T(8,128)(2,1)} copy(bf16[1,16,16,320]{3,2,1,0:T(8,128)(2,1)} %bitcast.11) | data formatting | bytes 327680
  89.9 1.6 %copy.14 = bf16[1,4,16,1280]{3,2,1,0:T(8,128)(2,1)} copy(bf16[1,4,16,1280]{3,2,1,0:T(8,128)(2,1)} %bitcast.12) | data formatting | bytes 327680

commit v3 on v2

--- a/solution.py
+++ b/solution.py
@@ -218,7 +218,6 @@
     y_out(0)
     for p in OTHER_TILES:
         project(p)
-    q_step(2)
 
     def spread_start(j):
         for k in range(1, NY):
@@ -304,6 +303,7 @@
 
     spread_start(0)
     lax.fori_loop(1, PER, lambda j, _: (y_out(j), 0)[1], 0)
+    q_step(2)
     spread_more(0)
     spread_start(1)
     q_step(3)
@@ -441,7 +441,7 @@
             dma((NY,)), dma((NY,)),
         ],
         compiler_params=pltpu.CompilerParams(
-            collective_id=0, has_side_effects=True, vmem_limit_bytes=63 * 2**20
+            collective_id=0, has_side_effects=True, vmem_limit_bytes=54 * 2**20
         ),
     )(
         control.reshape(TOK, C),

time: 91.6 us -> 91.6 us (level)
  no operation moved by 1% of the time
where the time goes in v3:
time: 91.6 us; the launch traced here: 91.4 us
  Pallas kernels  87.6 us (96%)
  local copies, waits for them, and re-layouts  3.22 us (4%)
    pallas_call x1, Pallas kernels, body(): pl.pallas_call(kernel, out_shape=[jax.ShapeDtypeStruct((TOK, C), BF16), j...  87.6 us
    unnamed x2, local copies, waits for them, and re-layouts  3.22 us

profile of v3, /device:TPU:8, one launch (start us, length us, event | category | flops | bytes accessed | tf_op | source)
XLA Modules:
  0.0 91.4 jit_solution(1489631022919772990)
XLA Ops:
  0.6 87.6 %shard_map.104 = (bf16[256,320]{1,0:T(8,128)(2,1)}, bf16[64,1280]{1,0:T(8,128)(2,1)}) custom-call(bf16[256,320]{1,0:T(8,128)(2,1)} %bitcast.10, bf16[9,320,320]{2,1,0:T(8,128)(2,1)} %bitcast.7, f32[320]{0:T(512)} %bias_h.1, bf16[320,320]{1,0:T(8,128)(2,1)} %zw_h.1, f32[8]{0:T(128)} %strg_h.1, s32[8]{0:T(128)} %bitcast.13, bf16[320,2560]{1,0:T(8,128)(2,1)} %wkv_h.1, ...), custom_call_target="tpu_custom_call" | custom-call | tf_op jit(solution)/shard_map/pallas_call | solution.py:402
  88.2 1.6 %copy.13 = bf16[1,16,16,320]{3,2,1,0:T(8,128)(2,1)} copy(bf16[1,16,16,320]{3,2,1,0:T(8,128)(2,1)} %bitcast.11) | data formatting | bytes 327680
  89.8 1.6 %copy.14 = bf16[1,4,16,1280]{3,2,1,0:T(8,128)(2,1)} copy(bf16[1,4,16,1280]{3,2,1,0:T(8,128)(2,1)} %bitcast.12) | data formatting | bytes 327680
